TPU v7x, 512 devices: a whole 4x4x16 slice. The times are simulated.
512 devices in a mesh: seq: 64 (over z, y_lo, core), kv: 8 (over y_hi, x).
Axes of the slice: x: 4, y: 4 (y_hi: 2, y_lo: 2; y = y_hi * 2 + y_lo), z: 16, core: 2. Of those that a mesh axis runs over, the one named last changes fastest.
Arguments:
- queries: bfloat16 [8192, 8192], P('seq', 'kv'), parts along dimension 1, may hold values from -4.5 to 4.5
- keys: bfloat16 [8192, 1024], P('seq', 'kv'), parts along dimension 1, may hold values from -4.5 to 4.5
- values: bfloat16 [8192, 1024], P('seq', 'kv'), parts along dimension 1, may hold values from -6 to 6
- block_order: int32 [128], replicated, may hold values from 0 to 127, each once
Outputs:
- attention: bfloat16 [8192, 8192], P('seq', 'kv'), parts along dimension 1
- row_lse: float32 [64, 8192], P('kv', 'seq'), parts along dimension 0
- column_sums: float32 [65536], P(('kv', 'seq')), parts along dimension 0
There are 8 independent parts, one for each index of `kv`. A program takes and returns all parts, laid end to end along the dimension named above; an argument that names none is the same for every part. Nothing has to cross between parts.
Inputs may be any that keep to these rules, and one draw needn't show every extreme that they name: `block_order`: every value of 0 to 127 appears once.
All inputs are finite; a program needn't handle non-finite values.
Results may differ from a plain program's by a relative error of at most 0.0047.
Values may be sent and summed in bfloat16 or wider, within the bound.
A program may use at most 64 MiB of HBM per device.

v0:
```python
import math
import jax
import jax.numpy as jnp
from jax import lax
from jax.sharding import PartitionSpec as P

BLOCK = 64
NEG_FILL = -1e30


def key_positions(block_order, first_row, count):
    row_ids = first_row + jnp.arange(count, dtype=jnp.int32)
    block_ids = row_ids // BLOCK
    one_hot = block_ids[:, None] == jnp.arange(block_order.shape[0], dtype=jnp.int32)[None, :]
    chosen = jnp.sum(jnp.where(one_hot, block_order[None, :], 0), axis=1)
    return chosen * BLOCK + row_ids % BLOCK


def tile_scores(query_heads, key_tile, query_pos, key_pos):
    factor = 1.0 / math.sqrt(key_tile.shape[1])
    scaled = (
        jnp.einsum("qhd,kd->hqk", query_heads, key_tile, preferred_element_type=jnp.float32)
        * factor
    )
    allowed = key_pos[None, :] <= query_pos[:, None]
    return jnp.where(allowed[None, :, :], scaled, NEG_FILL)


def over_tiles(update, carried, key_arrays, first_row, block_order):
    count = key_arrays[0].shape[0]
    width = math.gcd(count, 512)
    turns = count // width

    def one_turn(turn_index, running):
        offset = turn_index * width
        tiles = tuple((lax.dynamic_slice_in_dim(member, offset, width, 0) for member in key_arrays))
        key_pos = key_positions(block_order, first_row + offset, width)
        return update(running, tiles, key_pos, first_row + offset)

    return lax.fori_loop(0, turns, one_turn, carried)


def local(queries, keys, values, block_order):
    tok_rows = queries.shape[0]
    head_dim = keys.shape[1]
    head_count = queries.shape[1] // head_dim
    query_heads = queries.reshape(tok_rows, head_count, head_dim)
    own_first = lax.axis_index("seq") * tok_rows
    query_pos = key_positions(block_order, own_first, tok_rows)
    all_rows = tok_rows * lax.axis_size("seq")

    def stats_update(running, tiles, key_pos, first_row):
        top, total = running
        scores = tile_scores(query_heads, tiles[0], query_pos, key_pos)
        new_top = jnp.maximum(top, jnp.max(scores, axis=2))
        total = total * jnp.exp(top - new_top) + jnp.sum(
            jnp.exp(scores - new_top[:, :, None]), axis=2
        )
        return (new_top, total)

    def make_mix(row_lse):

        def mix_update(running, tiles, key_pos, first_row):
            accum, columns = running
            scores = tile_scores(query_heads, tiles[0], query_pos, key_pos)
            probs = jnp.exp(scores - row_lse[:, :, None])
            columns = lax.dynamic_update_slice_in_dim(
                columns, jnp.sum(probs, axis=(0, 1)), first_row, 0
            )
            accum = accum + jnp.einsum(
                "hqk,kd->qhd",
                probs.astype(jnp.bfloat16),
                tiles[1],
                preferred_element_type=jnp.float32,
            )
            return (accum, columns)

        return mix_update

    init_stats = (
        jnp.full((head_count, tok_rows), NEG_FILL, jnp.float32),
        jnp.zeros((head_count, tok_rows), jnp.float32),
    )
    init_mix = (
        jnp.zeros((tok_rows, head_count, head_dim), jnp.float32),
        jnp.zeros((all_rows,), jnp.float32),
    )
    whole_keys, whole_values = (
        lax.all_gather(keys, "seq", axis=0, tiled=True),
        lax.all_gather(values, "seq", axis=0, tiled=True),
    )
    top, total = over_tiles(stats_update, init_stats, (whole_keys,), 0, block_order)
    row_lse = top + jnp.log(total)
    accum, columns = over_tiles(
        make_mix(row_lse), init_mix, (whole_keys, whole_values), 0, block_order
    )
    attention = accum.reshape(tok_rows, head_count * head_dim).astype(jnp.bfloat16)
    column_sums = lax.psum_scatter(columns, "seq", scatter_dimension=0, tiled=True)
    return (attention, row_lse, column_sums)


def solution(mesh):
    placed = (P("seq", "kv"), P("seq", "kv"), P("seq", "kv"), P())
    return jax.shard_map(
        local,
        mesh=mesh,
        in_specs=placed,
        out_specs=(P("seq", "kv"), P("kv", "seq"), P(("kv", "seq"))),
        check_vma=False,
    )
```

profile of v0, /device:TPU:2, one launch (start us, length us, event | category | flops | bytes accessed | tf_op | source)
XLA Modules:
  0.0 545.5 jit_solution(4366825946389751583)
XLA Ops:
  7.9 1.5 copy.19
  13.6 123.1 %all-gather.5.cloned.1.call-done = bf16[8192,128]{1,0:T(8,128)(2,1)} async-done(((bf16[128,128]{1,0:T(8,128)(2,1)}), bf16[8192,128]{1,0:T(8,128)(2,1)}) %all-gather.5.cloned.1.call-update) | async-done | bytes 2097168 | tf_op jit(solution)/shard_map/all_gather | solution.py:89
  136.7 47.2 %while.36 = (s32[]{:T(128)}, f32[8,128]{1,0:T(8,128)S(1)}, f32[8,128]{1,0:T(8,128)S(1)}, s32[128]{0:T(128)}, s32[128]{0:T(128)S(1)}, /*index=5*/bf16[8192,128]{1...) while((s32[]{:T(128)}, f32[8,128]{1,0:T(8,128)S(1)}, ...), condition=%wide.region_5.6_spmd.clone, body=%wide.region_1.5_spmd.clone.sunk | while | flops 138169856 | bytes 4850866 | solution.py:40
  184.0 73.2 %all-gather.3.cloned.1.call-done = bf16[8192,128]{0,1:T(8,128)(2,1)} async-done(((bf16[128,128]{0,1:T(8,128)(2,1)}), bf16[8192,128]{0,1:T(8,128)(2,1)}) %all-gather.3.cloned.1.call-update) | async-done | bytes 2097168 | tf_op jit(solution)/shard_map/all_gather | solution.py:90
  257.1 70.1 %while.37 = (s32[]{:T(128)}, f32[128,8,128]{0,2,1:T(8,128)S(1)}, f32[8192]{0:T(1024)S(1)}, bf16[8192,128]{0,1:T(8,128)(2,1)}, s32[128]{0:T(128)}, /*index=5*/s32...) while((s32[]{:T(128)}, f32[128,8,128]{0,2,1:T(8,128)S(1)}, ...), condition=%wide.region_9.10_spmd.clone, body=%wide.region_6.9_spmd.clone.sunk | while | flops 271595520 | bytes 3824841 | solution.py:40
  258.2 1.6 fusion.47
  262.5 1.6 fusion.47
  264.2 1.4 fusion.48
  266.9 1.6 fusion.47
  268.5 1.4 fusion.48
  271.3 1.6 fusion.47
  272.9 1.4 fusion.48
  275.7 1.6 fusion.47
  277.3 1.4 fusion.48
  280.1 1.6 fusion.47
  281.7 1.4 fusion.48
  284.5 1.6 fusion.47
  286.1 1.4 fusion.48
  288.9 1.6 fusion.47
  290.5 1.4 fusion.48
  293.2 1.6 fusion.47
  297.6 1.6 fusion.47
  299.3 1.4 fusion.48
  302.0 1.6 fusion.47
  306.4 1.6 fusion.47
  310.8 1.6 fusion.47
  312.4 1.4 fusion.48
  315.2 1.6 fusion.47
  319.6 1.6 fusion.47
  321.2 1.4 fusion.48
  323.9 1.6 fusion.47
  328.2 209.9 %all-reduce = f32[8192]{0:T(1024)S(1)} all-reduce(f32[8192]{0:T(1024)S(1)} %get-tuple-element.410), channel_id=2, replica_groups=mesh['seq'=64,'kv'=8] {'seq'}, use_global_device_ids=true, to_apply=%region_10.11.clone | all-reduce | flops 8192 | bytes 65536
  (250 shorter events, 81.1 us)
Async XLA Ops:
  7.2 129.6 %all-gather.5.cloned.1.call-start = ((), (), s32[]{:S(2)}) async-start(), calls=%async_computation.1 | async-start | bytes 2129920 | tf_op jit(solution)/shard_map/all_gather | solution.py:89
  7.9 249.2 %all-gather.3.cloned.1.call-start = ((), (), s32[]{:S(2)}) async-start(), calls=%async_computation | async-start | bytes 2129920 | tf_op jit(solution)/shard_map/all_gather | solution.py:90
  327.3 211.4 %copy-start = (f32[8,128]{1,0:T(8,128)}, f32[8,128]{1,0:T(8,128)S(1)}, u32[]{:S(2)}) copy-start(f32[8,128]{1,0:T(8,128)S(1)} %get-tuple-element.741) | copy-start | bytes 12292
Sparse Core Ops, SparseCore 0:
  10.2 126.5 all-gather.4
  139.4 117.7 all-gather.2
where the time goes:
time: 547 us; the launch traced here: 546 us
  blocking collectives  210 us (38%)
  waiting for transfers between devices  197 us (36%)
  matrix products  70.7 us (13%)
  other arithmetic  41.4 us (8%)
  between operations  14.8 us (3%)
  local copies, waits for them, and re-layouts  9.99 us (2%)
    unnamed x1, blocking collectives  210 us
    all_gather x1, waiting for transfers between devices, local(): lax.all_gather(keys, 'seq', axis=0, tiled=True)  123 us
    all_gather x1, waiting for transfers between devices, local(): lax.all_gather(values, 'seq', axis=0, tiled=True)  73.2 us
    dot_general x32, matrix products, tile_scores(): jnp.einsum('qhd,kd->hqk', query_heads, key_tile, preferred_element_type=j...  47.6 us
    reduce_sum x33, other arithmetic, key_positions(): chosen = jnp.sum(jnp.where(one_hot, block_order[None, :], 0), axis=1)  29.2 us
    dot_general x16, matrix products, mix_update(): jnp.einsum('hqk,kd->qhd', probs.astype(jnp.bfloat16), tiles[1], preferred...  23.1 us
  transfers between devices with their start and end apart: 2, of which 2 were waited for; matrix products, arithmetic and copies ran while one was open for 9% of the time, Pallas kernels for 0%

commit v1 on v0

--- a/solution.py
+++ b/solution.py
@@ -1,11 +1,24 @@
+import functools
 import math
 import jax
 import jax.numpy as jnp
 from jax import lax
 from jax.sharding import PartitionSpec as P
+from jax.lax import all_to_all, axis_size
 
 BLOCK = 64
 NEG_FILL = -1e30
+
+
+def scan_rounds(piece_in, link_axis):
+    heard = all_to_all(
+        jnp.stack([piece_in for _ in range(axis_size(link_axis))], 0), link_axis, 0, 0
+    )
+    e_next = jnp.concatenate(heard, 0)
+    return e_next
+
+
+units_meet = functools.partial(scan_rounds, link_axis="seq")
 
 
 def key_positions(block_order, first_row, count):
@@ -85,10 +98,7 @@
         jnp.zeros((tok_rows, head_count, head_dim), jnp.float32),
         jnp.zeros((all_rows,), jnp.float32),
     )
-    whole_keys, whole_values = (
-        lax.all_gather(keys, "seq", axis=0, tiled=True),
-        lax.all_gather(values, "seq", axis=0, tiled=True),
-    )
+    whole_keys, whole_values = (units_meet(keys), lax.all_gather(values, "seq", axis=0, tiled=True))
     top, total = over_tiles(stats_update, init_stats, (whole_keys,), 0, block_order)
     row_lse = top + jnp.log(total)
     accum, columns = over_tiles(

time: 547 us -> 470 us (0.86)
  the two profiles are of different devices: /device:TPU:2 before, /device:TPU:4 now
where the time goes in v1:
time: 470 us; the launch traced here: 469 us
  blocking collectives  209 us (44%)
  waiting for transfers between devices  124 us (26%)
  matrix products  70.8 us (15%)
  other arithmetic  19.8 us (4%)
  starting transfers between devices  17.5 us (4%)
  between operations  14.7 us (3%)
  local copies, waits for them, and re-layouts  10.9 us (2%)
    unnamed x1, blocking collectives  209 us
    all_to_all x1, waiting for transfers between devices, scan_rounds(): all_to_all(jnp.stack([piece_in for _ in range(axis_size(link_axis))], 0),...  98.6 us
    dot_general x32, matrix products, tile_scores(): jnp.einsum('qhd,kd->hqk', query_heads, key_tile, preferred_element_type=j...  47.7 us
    all_gather x1, waiting for transfers between devices, local(): lax.all_gather(values, 'seq', axis=0, tiled=True)  25.3 us
    dot_general x16, matrix products, mix_update(): jnp.einsum('hqk,kd->qhd', probs.astype(jnp.bfloat16), tiles[1], preferred...  23.1 us
    all_to_all x1, starting transfers between devices, scan_rounds(): all_to_all(jnp.stack([piece_in for _ in range(axis_size(link_axis))], 0),...  17.5 us
  transfers between devices with their start and end apart: 2, of which 2 were waited for; matrix products, arithmetic and copies ran while one was open for 8% of the time, Pallas kernels for 0%

profile of v1, /device:TPU:4, one launch (start us, length us, event | category | flops | bytes accessed | tf_op | source)
XLA Modules:
  0.0 468.7 jit_solution(6222555116387486209)
XLA Ops:
  7.2 2.6 stack.2
  9.8 17.5 %all-to-all-start = ((bf16[64,128,128]{2,1,0:T(8,128)(2,1)}), bf16[64,128,128]{2,1,0:T(8,128)(2,1)}, u32[]{:S(2)}, u32[]{:S(2)}) async-start(bf16[64,128,128]{2,1,0:T(8,128)(2,1)} %stack.2), calls=%async_computation | async-start | bytes 4194304 | tf_op jit(solution)/shard_map/all_to_all | solution.py:14
  30.6 98.6 %all-to-all-done = bf16[64,128,128]{2,1,0:T(8,128)(2,1)} async-done(((bf16[64,128,128]{2,1,0:T(8,128)(2,1)}), bf16[64,128,128]{2,1,0:T(8,128)(2,1)}, u32[]{:S(2)}, u32[]{:S(2)}) %all-to-all-start) | async-done | bytes 2097184 | tf_op jit(solution)/shard_map/all_to_all | solution.py:14
  129.2 36.7 %while.36 = (s32[]{:T(128)}, f32[8,128]{1,0:T(8,128)S(1)}, f32[8,128]{1,0:T(8,128)S(1)}, s32[128]{0:T(128)S(1)}, s32[128]{0:T(128)S(1)}, /*index=5*/bf16[8192,12...) while((s32[]{:T(128)}, f32[8,128]{1,0:T(8,128)S(1)}, ...), condition=%wide.region_5.6_spmd.clone, body=%wide.region_1.5_spmd.clone.sunk | while | flops 138169856 | bytes 4850866 | solution.py:53
  165.9 25.3 %all-gather.2.cloned.1.call-done = bf16[8192,128]{0,1:T(8,128)(2,1)} async-done(((bf16[128,128]{0,1:T(8,128)(2,1)}), bf16[8192,128]{0,1:T(8,128)(2,1)}) %all-gather.2.cloned.1.call-update) | async-done | bytes 2097168 | tf_op jit(solution)/shard_map/all_gather | solution.py:101
  191.2 59.8 %while.37 = (s32[]{:T(128)}, f32[128,8,128]{0,2,1:T(8,128)S(1)}, f32[8192]{0:T(1024)S(1)}, bf16[8192,128]{0,1:T(8,128)(2,1)}, s32[128]{0:T(128)S(1)}, /*index=5*...) while((s32[]{:T(128)}, f32[128,8,128]{0,2,1:T(8,128)S(1)}, ...), condition=%wide.region_9.10_spmd.clone, body=%wide.region_6.9_spmd.clone.sunk | while | flops 271595520 | bytes 3824841 | solution.py:53
  191.6 1.6 fusion.47
  193.2 1.4 fusion.48
  195.3 1.6 fusion.47
  197.0 1.4 fusion.48
  199.1 1.6 fusion.47
  200.7 1.4 fusion.48
  202.8 1.6 fusion.47
  204.4 1.4 fusion.48
  206.6 1.6 fusion.47
  208.2 1.4 fusion.48
  210.3 1.6 fusion.47
  211.9 1.4 fusion.48
  214.0 1.6 fusion.47
  215.7 1.4 fusion.48
  217.8 1.6 fusion.47
  221.5 1.6 fusion.47
  225.3 1.6 fusion.47
  229.0 1.6 fusion.47
  232.7 1.6 fusion.47
  236.5 1.6 fusion.47
  240.2 1.6 fusion.47
  243.9 1.6 fusion.47
  245.6 1.4 fusion.48
  247.7 1.6 fusion.47
  249.3 1.4 fusion.48
  251.9 209.3 %all-reduce = f32[8192]{0:T(1024)S(1)} all-reduce(f32[8192]{0:T(1024)S(1)} %get-tuple-element.410), channel_id=2, replica_groups=mesh['seq'=64,'kv'=8] {'seq'}, use_global_device_ids=true, to_apply=%region_10.11.clone | all-reduce | flops 8192 | bytes 65536
  (256 shorter events, 60.1 us)
Async XLA Ops:
  9.8 17.6 %copy-start.2 = (bf16[128,128]{1,0:T(8,128)(2,1)S(1)}, bf16[128,128]{1,0:T(8,128)(2,1)}, u32[]{:S(2)}) copy-start(bf16[128,128]{1,0:T(8,128)(2,1)} %param.10) | copy-start | bytes 98308
  9.8 18.4 %copy-start = (bf16[128,1024]{1,0:T(8,128)(2,1)S(1)}, bf16[128,1024]{1,0:T(8,128)(2,1)}, u32[]{:S(2)}) copy-start(bf16[128,1024]{1,0:T(8,128)(2,1)} %param.8) | copy-start | bytes 786436
  9.8 20.6 %copy-start.1 = (s32[128]{0:T(128)S(1)}, s32[128]{0:T(128)}, u32[]{:S(2)}) copy-start(s32[128]{0:T(128)} %param.11) | copy-start | bytes 1540
  9.8 119.4 %all-to-all-start = ((bf16[64,128,128]{2,1,0:T(8,128)(2,1)}), bf16[64,128,128]{2,1,0:T(8,128)(2,1)}, u32[]{:S(2)}, u32[]{:S(2)}) async-start(bf16[64,128,128]{2,1,0:T(8,128)(2,1)} %stack.2), calls=%async_computation | async-start | bytes 4194304 | tf_op jit(solution)/shard_map/all_to_all | solution.py:14
  27.3 163.9 %all-gather.2.cloned.1.call-start = ((), (), s32[]{:S(2)}) async-start(), calls=%async_computation.1 | async-start | bytes 2129920 | tf_op jit(solution)/shard_map/all_gather | solution.py:101
  251.0 210.8 %copy-start.3 = (f32[8,128]{1,0:T(8,128)}, f32[8,128]{1,0:T(8,128)S(1)}, u32[]{:S(2)}) copy-start(f32[8,128]{1,0:T(8,128)S(1)} %get-tuple-element.736) | copy-start | bytes 12292
Sparse Core Ops, SparseCore 0:
  30.8 160.4 all-gather.1
